TPU v7x, 256 devices: a whole 4x4x8 slice. The times are simulated.
256 devices in a mesh: band: 128 (over z, y, x), tp: 2 (over core).
Axes of the slice: x: 4, y: 4, z: 8, core: 2. Of those that a mesh axis runs over, the one named last changes fastest.
Arguments:
- grid_input: bfloat16 [131072, 474], P('band'), may hold values from -6 to 6
- mesh_latent: bfloat16 [40960, 512], P('band'), may hold values from -6 to 6
- edge_latent: bfloat16 [327680, 512], P('band'), may hold values from -6 to 6
- slot_grid_row: int32 [384, 1024], P('band'), may hold values from 0 to 1024, as said below
- slot_mesh_row: int32 [384, 1024], P('band'), may hold values from 0 to 320, as said below
- halo_send: int32 [16384, 16], P('band'), may hold values from 0 to 320, as said below
- edge_sender: int32 [327680], P('band'), may hold values from 0 to 2367, as said below
- edge_receiver: int32 [327680], P('band'), may hold values from 0 to 319
- embed_in: bfloat16 [474, 512], P(None, 'tp'), may hold values from -0.25 to 0.25
- embed_out: bfloat16 [512, 512], P('tp'), may hold values from -0.25 to 0.25
- encode_sender: bfloat16 [512, 512], P(None, 'tp'), may hold values from -0.25 to 0.25
- encode_receiver: bfloat16 [512, 512], P(None, 'tp'), may hold values from -0.25 to 0.25
- encode_out: bfloat16 [512, 512], P('tp'), may hold values from -0.25 to 0.25
- encode_node_in: bfloat16 [1024, 512], P(None, 'tp'), may hold values from -0.1875 to 0.1875
- encode_node_out: bfloat16 [512, 512], P('tp'), may hold values from -0.25 to 0.25
- layer_sender: bfloat16 [2, 512, 512], P(None, None, 'tp'), may hold values from -0.25 to 0.25
- layer_receiver: bfloat16 [2, 512, 512], P(None, None, 'tp'), may hold values from -0.25 to 0.25
- layer_edge: bfloat16 [2, 512, 512], P(None, None, 'tp'), may hold values from -0.25 to 0.25
- layer_message: bfloat16 [2, 512, 512], P(None, 'tp'), may hold values from -0.25 to 0.25
- layer_node_in: bfloat16 [2, 1024, 512], P(None, None, 'tp'), may hold values from -0.1875 to 0.1875
- layer_node_out: bfloat16 [2, 512, 512], P(None, 'tp'), may hold values from -0.25 to 0.25
Outputs:
- mesh_result: bfloat16 [40960, 512], P('band')
Inputs may be any that keep to these rules, and one draw needn't show every extreme that they name: `slot_grid_row`: 1024 marks an empty slot; live slots of a block come first; block 0 of the first band and block 2 of the last are empty; every other block holds 256 to 1024 live slots, and in every draw all three blocks sending to some partition are full. `slot_mesh_row`: 320 marks an empty slot, exactly where the matching sending slot is empty. `halo_send`: 320 marks an empty slot; live slots come first; a partition sends nothing to itself; in every draw some partition receives 16 live slots from every other. `edge_sender`: a value s at or over 320 names slot (s - 320) % 16 sent by partition (s - 320) // 16 to this one, always a live slot.
All inputs are finite; a program needn't handle non-finite values.
Results may differ from a plain program's by a relative error of at most 0.028.
Values may be sent and summed in bfloat16 or wider, within the bound.
No kernel may reach another device: no remote copies, remote signals or barrier semaphores. Data moves between devices by JAX's collectives and lax.ppermute only.
A program may use at most 64 MiB of HBM per device.

v0:
```python
import jax
import jax.numpy as jnp
from jax import lax
from jax.sharding import PartitionSpec as P


def with_halo(block, sides, width):
    for axis, dim in sides:
        count = lax.axis_size(axis)
        forward = [(i, i + 1) for i in range(count - 1)]
        backward = [(target, source) for source, target in forward]
        low = lax.ppermute(
            lax.slice_in_dim(block, block.shape[dim] - width, None, axis=dim), axis, forward
        )
        high = lax.ppermute(lax.slice_in_dim(block, 0, width, axis=dim), axis, backward)
        block = jnp.concatenate([low, block, high], axis=dim)
    return block


def matmul(left, right):
    return jnp.dot(left, right, preferred_element_type=jnp.float32)


def normalize(values):
    centre = jnp.mean(values, axis=-1, keepdims=True)
    centered = values - centre
    variance = jnp.mean(centered * centered, axis=-1, keepdims=True)
    return centered * lax.rsqrt(variance + 1e-05)


def gather_sum(values, targets, count):
    onehot = (jnp.arange(count, dtype=jnp.int32)[:, None] == targets[None, :]).astype(jnp.bfloat16)
    return jnp.dot(onehot, values, preferred_element_type=jnp.float32)


def with_zero(table):
    return jnp.concatenate([table, jnp.zeros((1, table.shape[1]), table.dtype)], axis=0)


def node_update(latent, hidden, message_weight, first_weight, second_weight):
    width = latent.shape[1]
    message = lax.psum(matmul(hidden, message_weight).astype(jnp.bfloat16), "tp")
    inner = jax.nn.silu(
        matmul(latent, first_weight[:width]) + matmul(message, first_weight[width:])
    ).astype(jnp.bfloat16)
    total = lax.psum(matmul(inner, second_weight).astype(jnp.bfloat16), "tp").astype(jnp.float32)
    return (latent.astype(jnp.float32) + normalize(total)).astype(jnp.bfloat16)


def shards(
    grid_input,
    mesh_latent,
    edge_latent,
    slot_grid_row,
    slot_mesh_row,
    halo_send,
    edge_sender,
    edge_receiver,
    embed_in,
    embed_out,
    encode_sender,
    encode_receiver,
    encode_out,
    encode_node_in,
    encode_node_out,
    layer_sender,
    layer_receiver,
    layer_edge,
    layer_message,
    layer_node_in,
    layer_node_out,
):
    node_count = mesh_latent.shape[0]
    slot_count = slot_grid_row.shape[1]
    inner = jax.nn.silu(matmul(grid_input, embed_in)).astype(jnp.bfloat16)
    grid_latent = normalize(
        lax.psum(matmul(inner, embed_out).astype(jnp.bfloat16), "tp").astype(jnp.float32)
    ).astype(jnp.bfloat16)
    grid_proj = matmul(grid_latent, encode_sender).astype(jnp.bfloat16)
    mesh_proj = matmul(mesh_latent, encode_receiver).astype(jnp.bfloat16)
    grid_slots = slot_grid_row.reshape(-1)
    outgoing = jnp.take(with_zero(grid_proj), grid_slots, axis=0)
    widened = with_halo(outgoing, (("band", 0),), slot_count)
    incoming = jnp.concatenate(
        [widened[:slot_count], widened[2 * slot_count : 3 * slot_count], widened[4 * slot_count :]],
        axis=0,
    )
    targets = slot_mesh_row.reshape(-1)
    pre_act = incoming.astype(jnp.float32) + jnp.take(with_zero(mesh_proj), targets, axis=0).astype(
        jnp.float32
    )
    active = jax.nn.silu(pre_act).astype(jnp.bfloat16)
    hidden = gather_sum(active, targets, node_count).astype(jnp.bfloat16)
    latent = node_update(mesh_latent, hidden, encode_out, encode_node_in, encode_node_out)
    for layer_index in range(layer_sender.shape[0]):
        sender_weight = layer_sender[layer_index]
        local_proj = matmul(latent, sender_weight).astype(jnp.bfloat16)
        outgoing = jnp.take(with_zero(latent), halo_send, axis=0)
        arrived = lax.all_to_all(outgoing, "band", split_axis=0, concat_axis=0, tiled=True)
        far_proj = matmul(arrived.reshape(-1, latent.shape[1]), sender_weight).astype(jnp.bfloat16)
        sender_table = jnp.concatenate([local_proj, far_proj], axis=0)
        receiver_proj = matmul(latent, layer_receiver[layer_index]).astype(jnp.bfloat16)
        pre_act = (
            matmul(edge_latent, layer_edge[layer_index])
            + jnp.take(sender_table, edge_sender, axis=0).astype(jnp.float32)
            + jnp.take(receiver_proj, edge_receiver, axis=0).astype(jnp.float32)
        )
        active = jax.nn.silu(pre_act).astype(jnp.bfloat16)
        hidden = gather_sum(active, edge_receiver, node_count).astype(jnp.bfloat16)
        latent = node_update(
            latent,
            hidden,
            layer_message[layer_index],
            layer_node_in[layer_index],
            layer_node_out[layer_index],
        )
    return latent


def solution(mesh):
    return jax.shard_map(
        shards,
        mesh=mesh,
        in_specs=(
            P("band", None),
            P("band", None),
            P("band", None),
            P("band", None),
            P("band", None),
            P("band", None),
            P("band"),
            P("band"),
            P(None, "tp"),
            P("tp", None),
            P(None, "tp"),
            P(None, "tp"),
            P("tp", None),
            P(None, "tp"),
            P("tp", None),
            P(None, None, "tp"),
            P(None, None, "tp"),
            P(None, None, "tp"),
            P(None, "tp", None),
            P(None, None, "tp"),
            P(None, "tp", None),
        ),
        out_specs=P("band", None),
        check_vma=False,
    )
```

profile of v0, /device:TPU:1, one launch (start us, length us, event | category | flops | bytes accessed | tf_op | source)
XLA Modules:
  0.0 488.2 jit_solution(6722694290539245472)
XLA Ops:
  6.5 3.7 convolution_convert_fusion.2
  10.5 34.9 %all-reduce.12.cloned.1.call-done = bf16[1024,512]{1,0:T(8,128)(2,1)} async-done(((bf16[1024,512]{1,0:T(8,128)(2,1)}), bf16[1024,512]{1,0:T(8,128)(2,1)}) %all-reduce.12.cloned.1.call-update) | async-done | bytes 1048592 | tf_op jit(solution)/shard_map/psum | solution.py:77
  45.3 1.5 convert_reduce_fusion
  46.9 1.7 fusion.7
  48.6 0.5 convolution_convert_fusion.3
  49.1 13.0 %gather_fusion = bf16[3072,256]{1,0:T(8,128)(2,1)} fusion(bf16[1025,256]{1,0:T(8,128)(2,1)S(1)} %concatenate.21, s32[3072]{0:T(1024)S(1)} %broadcast_clamp_fusion.1), kind=kCustom, calls=%fused_computation.6 | custom fusion | bytes 3158016 | tf_op jit(solution)/shard_map/jit(_take)/gather | solution.py:82
  62.1 2.7 broadcast_select_fusion.2
  64.9 1.2 fusion.91
  66.1 3.6 collective-permute-start
  69.7 1.3 collective-permute-start.1
  71.0 0.2 convolution_convert_fusion.14
  71.4 13.0 %gather_fusion.1 = bf16[3072,256]{1,0:T(8,128)(2,1)} fusion(bf16[321,256]{1,0:T(8,128)(2,1)S(1)} %concatenate.23, s32[3072]{0:T(1024)S(1)} %broadcast_clamp_fusion), kind=kCustom, calls=%fused_computation.7 | custom fusion | bytes 3158016 | tf_op jit(solution)/shard_map/jit(_take)/gather | solution.py:89
  84.3 0.6 collective-permute-done.1
  84.9 4.7 convolution_convert_fusion.9
  89.7 1.2 fusion.72
  90.9 33.8 %all-reduce.14.cloned.1.call-done = bf16[320,512]{1,0:T(8,128)(2,1)} async-done(((bf16[320,512]{1,0:T(8,128)(2,1)}), bf16[320,512]{1,0:T(8,128)(2,1)}) %all-reduce.14.cloned.1.call-update) | async-done | bytes 327696 | tf_op jit(solution)/shard_map/psum | solution.py:42
  124.7 2.4 convolution_convert_fusion.8
  127.2 0.1 copy.25
  127.3 0.1 reshape.228
  127.4 0.1 copy.24
  127.5 30.3 %all-reduce.16.cloned.1.call-done = bf16[320,512]{1,0:T(8,128)(2,1)} async-done(((bf16[320,512]{1,0:T(8,128)(2,1)}), bf16[320,512]{1,0:T(8,128)(2,1)}) %all-reduce.16.cloned.1.call-update) | async-done | bytes 327696 | tf_op jit(solution)/shard_map/psum | solution.py:46
  157.8 1.1 convert_reduce_fusion.3
  158.9 1.2 fusion.32
  160.2 1.2 fusion.34
  161.4 9.2 %gather_fusion.2 = bf16[2048,512]{1,0:T(8,128)(2,1)} fusion(bf16[321,512]{1,0:T(8,128)(2,1)S(1)} %concatenate.24, s32[2048]{0:T(1024)S(1)} %broadcast_clamp_fusion.2), kind=kCustom, calls=%fused_computation.clone | custom fusion | bytes 4202496 | tf_op jit(solution)/shard_map/jit(_take)/gather | solution.py:98
  170.6 2.8 broadcast_select_fusion.1
  173.4 14.2 %all-to-all-start = ((bf16[128,16,512]{2,1,0:T(8,128)(2,1)}), bf16[128,16,512]{2,1,0:T(8,128)(2,1)}, u32[]{:S(2)}, u32[]{:S(2)}) async-start(bf16[128,16,512]{2,1,0:T(8,128)(2,1)} %broadcast_select_fusion.1), calls=%async_computation | async-start | bytes 4194304 | tf_op jit(solution)/shard_map/all_to_all | solution.py:99
  187.6 0.2 all-reduce.18.cloned.1.call-start
  187.9 1.2 convolution_convert_fusion.12
  189.1 8.1 %gather_fusion.4 = bf16[2560,256]{1,0:T(8,128)(2,1)} fusion(bf16[320,256]{1,0:T(8,128)(2,1)S(1)} %convolution_convert_fusion.12, s32[3072]{0:T(1024)S(1)} %pad_clamp_fusion), kind=kCustom, calls=%fused_computation.2.clone | custom fusion | bytes 2631680 | tf_op jit(solution)/shard_map/jit(_take)/gather | solution.py:106
  197.3 1.2 convolution_convert_fusion.13
  198.5 38.9 %all-to-all-done = bf16[128,16,512]{2,1,0:T(8,128)(2,1)} async-done(((bf16[128,16,512]{2,1,0:T(8,128)(2,1)}), bf16[128,16,512]{2,1,0:T(8,128)(2,1)}, u32[]{:S(2)}, u32[]{:S(2)}) %all-to-all-start) | async-done | bytes 2097184 | tf_op jit(solution)/shard_map/all_to_all | solution.py:99
  237.4 2.3 convolution_convert_fusion.1
  239.7 1.1 pad_maximum_fusion
  240.8 8.2 %gather_fusion.3 = bf16[2560,256]{1,0:T(8,128)(2,1)} fusion(bf16[2368,256]{1,0:T(8,128)(2,1)} %pad_maximum_fusion, s32[3072]{0:T(1024)S(1)} %pad_clamp_fusion.1), kind=kCustom, calls=%fused_computation.1.clone | custom fusion | bytes 2631680 | tf_op jit(solution)/shard_map/jit(_take)/gather | solution.py:105
  249.0 4.8 multiply_convert_fusion.2
  253.9 3.0 convolution_convert_fusion.7
  256.9 1.2 fusion.54
  258.1 25.9 %all-reduce.18.cloned.1.call-done = bf16[320,512]{1,0:T(8,128)(2,1)} async-done(((bf16[320,512]{1,0:T(8,128)(2,1)}), bf16[320,512]{1,0:T(8,128)(2,1)}) %all-reduce.18.cloned.1.call-update) | async-done | bytes 327696 | tf_op jit(solution)/shard_map/psum | solution.py:42
  284.0 2.4 convolution_convert_fusion.6
  286.5 30.6 %all-reduce.20.cloned.1.call-done = bf16[320,512]{1,0:T(8,128)(2,1)} async-done(((bf16[320,512]{1,0:T(8,128)(2,1)}), bf16[320,512]{1,0:T(8,128)(2,1)}) %all-reduce.20.cloned.1.call-update) | async-done | bytes 327696 | tf_op jit(solution)/shard_map/psum | solution.py:46
  317.1 1.1 convert_reduce_fusion.2
  318.2 1.2 fusion.29
  319.4 1.2 fusion.31
  320.6 0.7 copy-done.1
  321.4 9.2 %gather_fusion.5 = bf16[2048,512]{1,0:T(8,128)(2,1)} fusion(bf16[321,512]{1,0:T(8,128)(2,1)S(1)} %concatenate.26, s32[2048]{0:T(1024)S(1)} %broadcast_clamp_fusion.2), kind=kCustom, calls=%fused_computation.3.clone | custom fusion | bytes 4202496 | tf_op jit(solution)/shard_map/jit(_take)/gather | solution.py:98
  330.5 2.8 broadcast_select_fusion
  333.3 14.2 %all-to-all-start.1 = ((bf16[128,16,512]{2,1,0:T(8,128)(2,1)}), bf16[128,16,512]{2,1,0:T(8,128)(2,1)}, u32[]{:S(2)}, u32[]{:S(2)}) async-start(bf16[128,16,512]{2,1,0:T(8,128)(2,1)} %broadcast_select_fusion), calls=%async_computation.1 | async-start | bytes 4194304 | tf_op jit(solution)/shard_map/all_to_all | solution.py:99
  347.6 1.2 convolution_convert_fusion.10
  348.8 8.1 %gather_fusion.7 = bf16[2560,256]{1,0:T(8,128)(2,1)} fusion(bf16[320,256]{1,0:T(8,128)(2,1)S(1)} %convolution_convert_fusion.10, s32[3072]{0:T(1024)S(1)} %pad_clamp_fusion), kind=kCustom, calls=%fused_computation.5.clone | custom fusion | bytes 2631680 | tf_op jit(solution)/shard_map/jit(_take)/gather | solution.py:106
  357.0 1.2 convolution_convert_fusion.11
  358.2 39.1 %all-to-all-done.1 = bf16[128,16,512]{2,1,0:T(8,128)(2,1)} async-done(((bf16[128,16,512]{2,1,0:T(8,128)(2,1)}), bf16[128,16,512]{2,1,0:T(8,128)(2,1)}, u32[]{:S(2)}, u32[]{:S(2)}) %all-to-all-start.1) | async-done | bytes 2097184 | tf_op jit(solution)/shard_map/all_to_all | solution.py:99
  397.3 2.3 convolution_convert_fusion
  399.6 1.1 pad_maximum_fusion.1
  400.7 8.2 %gather_fusion.6 = bf16[2560,256]{1,0:T(8,128)(2,1)} fusion(bf16[2368,256]{1,0:T(8,128)(2,1)} %pad_maximum_fusion.1, s32[3072]{0:T(1024)S(1)} %pad_clamp_fusion.1), kind=kCustom, calls=%fused_computation.4.clone | custom fusion | bytes 2631680 | tf_op jit(solution)/shard_map/jit(_take)/gather | solution.py:105
  409.0 4.8 multiply_convert_fusion.1
  413.8 3.0 convolution_convert_fusion.5
  416.8 1.2 fusion.44
  418.0 25.9 %all-reduce.22.cloned.1.call-done = bf16[320,512]{1,0:T(8,128)(2,1)} async-done(((bf16[320,512]{1,0:T(8,128)(2,1)}), bf16[320,512]{1,0:T(8,128)(2,1)}) %all-reduce.22.cloned.1.call-update) | async-done | bytes 327696 | tf_op jit(solution)/shard_map/psum | solution.py:42
  444.0 2.4 convolution_convert_fusion.4
  446.4 30.6 %all-reduce.24.cloned.1.call-done = bf16[320,512]{1,0:T(8,128)(2,1)} async-done(((bf16[320,512]{1,0:T(8,128)(2,1)}), bf16[320,512]{1,0:T(8,128)(2,1)}) %all-reduce.24.cloned.1.call-update) | async-done | bytes 327696 | tf_op jit(solution)/shard_map/psum | solution.py:46
  477.0 1.1 convert_reduce_fusion.1
  478.2 1.2 fusion.26
  479.4 1.9 fusion.28
  (69 shorter events, 0.7 us)
Async XLA Ops:
  6.5 242.5 %copy-start = (bf16[2560,512]{1,0:T(8,128)(2,1)S(1)}, bf16[2560,512]{1,0:T(8,128)(2,1)}, u32[]{:S(2)}) copy-start(bf16[2560,512]{1,0:T(8,128)(2,1)} %param.29) | copy-start | bytes 7864324
  6.5 3.8 copy-start.6
  6.5 3.8 copy-start.7
  6.5 38.8 %all-reduce.12.cloned.1.call-start = ((), (), s32[]{:S(2)}) async-start(), calls=%async_computation.2 | async-start | bytes 2097152 | tf_op jit(solution)/shard_map/psum | solution.py:77
  10.2 38.4 %copy-start.11 = (bf16[512,256]{1,0:T(8,128)(2,1)S(1)}, bf16[512,256]{1,0:T(8,128)(2,1)}, u32[]{:S(2)}) copy-start(bf16[512,256]{1,0:T(8,128)(2,1)} %param.37) | copy-start | bytes 786436
  10.3 114.5 %all-reduce.14.cloned.1.call-start = ((), (), s32[]{:S(2)}) async-start(), calls=%async_computation.3 | async-start | bytes 655360 | tf_op jit(solution)/shard_map/psum | solution.py:42
  45.3 3.3 copy-start.3
  64.8 6.2 %copy-start.4 = (bf16[320,512]{1,0:T(8,128)(2,1)S(1)}, bf16[320,512]{1,0:T(8,128)(2,1)}, u32[]{:S(2)}) copy-start(bf16[320,512]{1,0:T(8,128)(2,1)} %param.28) | copy-start | bytes 983044
  64.8 6.2 %copy-start.5 = (bf16[512,256]{1,0:T(8,128)(2,1)S(1)}, bf16[512,256]{1,0:T(8,128)(2,1)}, u32[]{:S(2)}) copy-start(bf16[512,256]{1,0:T(8,128)(2,1)} %param.38) | copy-start | bytes 786436
  66.1 18.2 %collective-permute-start = (bf16[1024,256]{1,0:T(8,128)(2,1)}, bf16[1024,256]{1,0:T(8,128)(2,1)}, u32[]{:S(2)}, u32[]{:S(2)}) collective-permute-start(bf16[1024,256]{1,0:T(8,128)(2,1)} %get-tuple-element.6), channel_id=1, source_target_pairs={{0,2},{2,4},{4,6},{6,8},{8,10},{10,12},{12,14},{14,16},{16,18},{18... | collective-permute-start | bytes 1572872 | tf_op jit(solution)/shard_map/ppermute | solution.py:12
  69.7 15.2 %collective-permute-start.1 = (bf16[1024,256]{1,0:T(8,128)(2,1)}, bf16[1024,256]{1,0:T(8,128)(2,1)}, u32[]{:S(2)}, u32[]{:S(2)}) collective-permute-start(bf16[1024,256]{1,0:T(8,128)(2,1)} %get-tuple-element.8), channel_id=1, source_target_pairs={{2,0},{4,2},{6,4},{8,6},{10,8},{12,10},{14,12},{16,14},{18,16},{20... | collective-permute-start | bytes 1572872 | tf_op jit(solution)/shard_map/ppermute | solution.py:15
  71.3 13.6 %copy-start.12 = (bf16[256,512]{1,0:T(8,128)(2,1)S(1)}, bf16[256,512]{1,0:T(8,128)(2,1)}, u32[]{:S(2)}) copy-start(bf16[256,512]{1,0:T(8,128)(2,1)} %param.39) | copy-start | bytes 786436
  84.9 4.8 copy-start.10
  89.6 68.2 %all-reduce.16.cloned.1.call-start = ((), (), s32[]{:S(2)}) async-start(), calls=%async_computation.4 | async-start | bytes 655360 | tf_op jit(solution)/shard_map/psum | solution.py:46
  173.4 14.5 %copy-start.8 = (s32[2560]{0:T(1024)S(1)}, s32[2560]{0:T(1024)}, u32[]{:S(2)}) copy-start(s32[2560]{0:T(1024)} %param.33) | copy-start | bytes 30724
  173.4 14.5 %copy-start.9 = (s32[2560]{0:T(1024)S(1)}, s32[2560]{0:T(1024)}, u32[]{:S(2)}) copy-start(s32[2560]{0:T(1024)} %param.34) | copy-start | bytes 30724
  173.4 64.0 %all-to-all-start = ((bf16[128,16,512]{2,1,0:T(8,128)(2,1)}), bf16[128,16,512]{2,1,0:T(8,128)(2,1)}, u32[]{:S(2)}, u32[]{:S(2)}) async-start(bf16[128,16,512]{2,1,0:T(8,128)(2,1)} %broadcast_select_fusion.1), calls=%async_computation | async-start | bytes 4194304 | tf_op jit(solution)/shard_map/all_to_all | solution.py:99
  187.6 96.4 %all-reduce.18.cloned.1.call-start = ((), (), s32[]{:S(2)}) async-start(), calls=%async_computation.5 | async-start | bytes 655360 | tf_op jit(solution)/shard_map/psum | solution.py:42
  256.9 60.2 %all-reduce.20.cloned.1.call-start = ((), (), s32[]{:S(2)}) async-start(), calls=%async_computation.6 | async-start | bytes 655360 | tf_op jit(solution)/shard_map/psum | solution.py:46
  320.6 0.7 copy-start.1
  333.3 14.3 %copy-start.2 = (bf16[320,512]{1,0:T(8,128)(2,1)S(1)}, bf16[320,512]{1,0:T(8,128)(2,1)}, u32[]{:S(2)}) copy-start(bf16[320,512]{1,0:T(8,128)(2,1)} %copy-done.1) | copy-start | bytes 983044
  333.3 64.0 %all-to-all-start.1 = ((bf16[128,16,512]{2,1,0:T(8,128)(2,1)}), bf16[128,16,512]{2,1,0:T(8,128)(2,1)}, u32[]{:S(2)}, u32[]{:S(2)}) async-start(bf16[128,16,512]{2,1,0:T(8,128)(2,1)} %broadcast_select_fusion), calls=%async_computation.1 | async-start | bytes 4194304 | tf_op jit(solution)/shard_map/all_to_all | solution.py:99
  347.6 96.4 %all-reduce.22.cloned.1.call-start = ((), (), s32[]{:S(2)}) async-start(), calls=%async_computation.7 | async-start | bytes 655360 | tf_op jit(solution)/shard_map/psum | solution.py:42
  416.8 60.2 %all-reduce.24.cloned.1.call-start = ((), (), s32[]{:S(2)}) async-start(), calls=%async_computation.8 | async-start | bytes 655360 | tf_op jit(solution)/shard_map/psum | solution.py:46
Sparse Core Ops, SparseCore 0:
  10.4 34.9 all-reduce.11
  89.8 34.9 all-reduce.13
  127.3 30.4 all-reduce.15
  257.0 27.0 all-reduce.17
  286.6 30.4 all-reduce.19
  416.9 27.0 all-reduce.21
  446.6 30.4 all-reduce.23
where the time goes:
time: 490 us; the launch traced here: 488 us
  waiting for transfers between devices  291 us (59%)
  local copies, waits for them, and re-layouts  79.5 us (16%)
  matrix products  44.8 us (9%)
  starting transfers between devices  33.8 us (7%)
  other arithmetic  25.3 us (5%)
  between operations  13.9 us (3%)
    psum x3, waiting for transfers between devices, node_update(): lax.psum(matmul(inner, second_weight).astype(jnp.bfloat16), 'tp')  91.6 us
    psum x3, waiting for transfers between devices, node_update(): lax.psum(matmul(hidden, message_weight).astype(jnp.bfloat16), 'tp')  85.7 us
    all_to_all x2, waiting for transfers between devices, shards(): lax.all_to_all(outgoing, 'band', split_axis=0, concat_axis=0, tiled=True)  78 us
    dot_general x20, matrix products, matmul(): return jnp.dot(left, right, preferred_element_type=jnp.float32)  44.8 us
    psum x1, waiting for transfers between devices, shards(): lax.psum(matmul(inner, embed_out).astype(jnp.bfloat16), 'tp')  34.9 us
    all_to_all x2, starting transfers between devices, shards(): lax.all_to_all(outgoing, 'band', split_axis=0, concat_axis=0, tiled=True)  28.5 us
    gather x2, local copies, waits for them, and re-layouts, shards(): outgoing = jnp.take(with_zero(latent), halo_send, axis=0)  18.3 us
    gather x2, local copies, waits for them, and re-layouts, shards(): jnp.take(sender_table, edge_sender, axis=0).astype(jnp.float32)  16.5 us
  transfers between devices with their start and end apart: 11, of which 10 were waited for; matrix products, arithmetic and copies ran while one was open for 8% of the time, Pallas kernels for 0%

commit v1 on v0

v1 whole, which is shorter than its diff:
```python
import functools

import jax
import jax.numpy as jnp
from jax import lax
from jax.experimental import pallas as pl
from jax.experimental.pallas import tpu as pltpu
from jax.sharding import PartitionSpec as P

BF16 = jnp.bfloat16
F32 = jnp.float32


def matmul(left, right):
    return jnp.dot(left, right, preferred_element_type=F32)


def silu(values):
    half = 0.5 * values
    return half + half * jnp.tanh(half)


def normalize(values):
    centre = jnp.mean(values, axis=-1, keepdims=True)
    centered = values - centre
    variance = jnp.mean(centered * centered, axis=-1, keepdims=True)
    return centered * lax.rsqrt(variance + 1e-05)


def as_column(row):
    return jnp.transpose(jnp.broadcast_to(row, (128, row.shape[1])))


def pick_rows(column, count):
    n = column.shape[0]
    wide = jnp.concatenate([column] * pl.cdiv(count, 128), axis=1)[:, :count]
    lanes = lax.broadcasted_iota(jnp.int32, (n, count), 1)
    return jnp.where(wide == lanes, 1.0, 0.0).astype(BF16)


def pick_columns(row, count):
    n = row.shape[1]
    rows = lax.broadcasted_iota(jnp.int32, (count, n), 0)
    return jnp.where(row == rows, 1.0, 0.0).astype(BF16)


def call(kernel, outs, *args):
    return pl.pallas_call(
        kernel,
        out_shape=[jax.ShapeDtypeStruct(shape, dtype) for shape, dtype in outs],
        in_specs=[pl.BlockSpec(memory_space=pltpu.VMEM)] * len(args),
        out_specs=[pl.BlockSpec(memory_space=pltpu.VMEM)] * len(outs),
        compiler_params=pltpu.CompilerParams(vmem_limit_bytes=48 * 1024 * 1024),
    )(*args)


def embed_kernel(
    x_ref, in_own, in_other, out_own, out_other, sender_w, slots, low_ref, mid_ref, high_ref
):
    rows = x_ref.shape[0]
    x = x_ref[...]
    own = silu(matmul(x, in_own[...])).astype(BF16)
    other = silu(matmul(x, in_other[...])).astype(BF16)
    total = matmul(own, out_own[...]) + matmul(other, out_other[...])
    latent = normalize(total).astype(BF16)
    proj = matmul(latent, sender_w[...]).astype(BF16)
    for block, out in enumerate((low_ref, mid_ref, high_ref)):
        index = as_column(slots[block : block + 1, :])
        out[...] = matmul(pick_rows(index, rows), proj).astype(BF16)


def join(incoming, row, mesh_proj):
    count = mesh_proj.shape[0]
    pre_act = incoming.astype(F32) + matmul(pick_rows(as_column(row), count), mesh_proj)
    return matmul(pick_columns(row, count), silu(pre_act).astype(BF16))


def encode_mid_kernel(latent, receiver_w, slots, mid, proj_ref, sum_ref):
    proj = matmul(latent[...], receiver_w[...]).astype(BF16)
    proj_ref[...] = proj
    sum_ref[...] = join(mid[...], slots[1:2, :], proj)


def encode_far_kernel(proj, partial, slots, low, high, hidden_ref):
    table = proj[...]
    total = partial[...] + join(low[...], slots[0:1, :], table)
    total = total + join(high[...], slots[2:3, :], table)
    hidden_ref[...] = total.astype(BF16)


def node_kernel(more, latent, hidden_own, hidden_other, msg_own, msg_other, first_own, first_other,
                second_own, second_other, *refs):
    width = latent.shape[1]
    message = (
        matmul(hidden_own[...], msg_own[...]) + matmul(hidden_other[...], msg_other[...])
    ).astype(BF16)
    total = None
    for first, second in ((first_own, second_own), (first_other, second_other)):
        inner = silu(matmul(latent[...], first[:width, :]) + matmul(message, first[width:, :]))
        part = matmul(inner.astype(BF16), second[...])
        total = part if total is None else total + part
    new = (latent[...].astype(F32) + normalize(total)).astype(BF16)
    if not more:
        refs[0][...] = new
        return
    sender_w, receiver_w, halo, new_ref, local_ref, receiver_ref, outgoing_ref = refs
    new_ref[...] = new
    local = matmul(new, sender_w[...]).astype(BF16)
    local_ref[...] = local
    slots = halo.shape[1]
    outgoing_ref[...] = matmul(pick_rows(as_column(halo[...]), local.shape[0]), local).astype(BF16)
    receiver_ref[...] = matmul(new, receiver_w[...]).astype(BF16)


def edge_kernel(chunk, edges, edge_w, local, arrived, receiver_proj, senders, receivers, hidden_ref):
    count = local.shape[0]
    far = arrived.shape[0]
    total = None
    for start in range(0, edges.shape[0], chunk):
        sender = senders[:, start : start + chunk]
        receiver = receivers[:, start : start + chunk]
        column = as_column(sender)
        pre_act = matmul(edges[start : start + chunk, :], edge_w[...])
        pre_act += matmul(pick_rows(column - count, far), arrived[...])
        pre_act += matmul(pick_rows(column, count), local[...])
        pre_act += matmul(pick_rows(as_column(receiver), count), receiver_proj[...])
        part = matmul(pick_columns(receiver, count), silu(pre_act).astype(BF16))
        total = part if total is None else total + part
    hidden_ref[...] = total.astype(BF16)


def swap(values):
    return lax.ppermute(values, "tp", [(0, 1), (1, 0)])


def shards(
    grid_input,
    mesh_latent,
    edge_latent,
    slot_grid_row,
    slot_mesh_row,
    halo_send,
    edge_sender,
    edge_receiver,
    embed_in,
    embed_out,
    encode_sender,
    encode_receiver,
    encode_out,
    encode_node_in,
    encode_node_out,
    layer_sender,
    layer_receiver,
    layer_edge,
    layer_message,
    layer_node_in,
    layer_node_out,
):
    nodes, width = mesh_latent.shape
    slot_count = slot_grid_row.shape[1]
    half = encode_sender.shape[1]
    bands, halo_slots = halo_send.shape
    layers = layer_sender.shape[0]
    halo_row = halo_send.reshape(1, -1)
    sender_row = edge_sender.reshape(1, -1)
    receiver_row = edge_receiver.reshape(1, -1)

    slots_out = [((slot_count, half), BF16)] * 3
    low, mid, high = call(
        embed_kernel, slots_out, grid_input, embed_in, swap(embed_in), embed_out, swap(embed_out),
        encode_sender, slot_grid_row,
    )
    up = [(i, i + 1) for i in range(bands - 1)]
    down = [(i + 1, i) for i in range(bands - 1)]
    from_low = lax.ppermute(high, "band", up)
    from_high = lax.ppermute(low, "band", down)
    proj, partial = call(
        encode_mid_kernel, [((nodes, half), BF16), ((nodes, half), F32)],
        mesh_latent, encode_receiver, slot_mesh_row, mid,
    )
    (hidden,) = call(
        encode_far_kernel, [((nodes, half), BF16)], proj, partial, slot_mesh_row, from_low, from_high
    )

    def update(latent, hidden, message, first, second, following):
        args = (latent, hidden, swap(hidden), message, swap(message), first, swap(first), second,
                swap(second))
        outs = [((nodes, width), BF16)]
        if following:
            args += following
            outs += [((nodes, half), BF16)] * 2 + [((bands * halo_slots, half), BF16)]
        return call(functools.partial(node_kernel, bool(following)), outs, *args)

    message, first, second = encode_out, encode_node_in, encode_node_out
    latent = mesh_latent
    for layer in range(layers):
        latent, local, receiver_proj, outgoing = update(
            latent, hidden, message, first, second,
            (layer_sender[layer], layer_receiver[layer], halo_row),
        )
        arrived = lax.all_to_all(
            outgoing.reshape(bands, halo_slots, half), "band", split_axis=0, concat_axis=0, tiled=True
        ).reshape(bands * halo_slots, half)
        (hidden,) = call(
            functools.partial(edge_kernel, 512), [((nodes, half), BF16)], edge_latent,
            layer_edge[layer], local, arrived, receiver_proj, sender_row, receiver_row,
        )
        message, first, second = layer_message[layer], layer_node_in[layer], layer_node_out[layer]
    (latent,) = update(latent, hidden, message, first, second, ())
    return latent


def solution(mesh):
    return jax.shard_map(
        shards,
        mesh=mesh,
        in_specs=(
            P("band", None),
            P("band", None),
            P("band", None),
            P("band", None),
            P("band", None),
            P("band", None),
            P("band"),
            P("band"),
            P(None, "tp"),
            P("tp", None),
            P(None, "tp"),
            P(None, "tp"),
            P("tp", None),
            P(None, "tp"),
            P("tp", None),
            P(None, None, "tp"),
            P(None, None, "tp"),
            P(None, None, "tp"),
            P(None, "tp", None),
            P(None, None, "tp"),
            P(None, "tp", None),
        ),
        out_specs=P("band", None),
        check_vma=False,
    )
```

time: 490 us -> 168 us (0.34)
  waiting for transfers between devices: 291 us -> 61.7 us
  local copies, waits for them, and re-layouts: 79.5 us -> 27.3 us
  matrix products: 44.8 us -> 0 us
  Pallas kernels: 0 us -> 33.9 us
  other arithmetic: 25.3 us -> 0 us
  between operations: 13.9 us -> 0.3 us
  starting transfers between devices: 33.8 us -> 44.4 us
    psum x7 -> x0, waiting for transfers between devices: 212 us -> none  [the longest x3 91.6 us: node_update(): lax.psum(matmul(inner, second_weight).astype(jnp.bfloat16), 'tp')]
    gather x8 -> x0, local copies, waits for them, and re-layouts: 77 us -> none  [the longest x2 18.3 us: shards(): outgoing = jnp.take(with_zero(latent), halo_send, axis=0)]
    dot_general x20 -> x0, matrix products: 44.8 us -> none  [matmul(): return jnp.dot(left, right, preferred_element_type=jnp.float32)]
    pallas_call x0 -> x8, Pallas kernels: none -> 33.9 us  [call(): pl.pallas_call(kernel, out_shape=[jax.ShapeDtypeStruct(shape, dtype) for...]
    all_to_all x2, waiting for transfers between devices: 78 us -> 49.9 us  [shards(): lax.all_to_all(outgoing.reshape(bands, halo_slots, half), 'band', split_a...]
    unnamed x28 -> x84, local copies, waits for them, and re-layouts: 0.8 us -> 19.9 us
    ppermute x2 -> x16, starting transfers between devices: 4.92 us -> 17.1 us  [the longest x14 14.3 us: swap(): return lax.ppermute(values, 'tp', [(0, 1), (1, 0)])]
    ppermute x2 -> x16, waiting for transfers between devices: 0.58 us -> 11.7 us  [the longest x1 5.68 us: shards(): from_low = lax.ppermute(high, 'band', up)]
  transfers between devices with their start and end apart: 11 -> 18, of which waited for: 10 -> 8; matrix products, arithmetic and copies ran while one was open for 8% -> 6% of each run, Pallas kernels for 0% -> 11%
where the time goes in v1:
time: 168 us
  waiting for transfers between devices  61.7 us (37%)
  starting transfers between devices  44.4 us (26%)
  Pallas kernels  33.9 us (20%)
  local copies, waits for them, and re-layouts  27.3 us (16%)
    all_to_all x2, waiting for transfers between devices, shards(): lax.all_to_all(outgoing.reshape(bands, halo_slots, half), 'band', split_a...  49.9 us
    pallas_call x8, Pallas kernels, call(): pl.pallas_call(kernel, out_shape=[jax.ShapeDtypeStruct(shape, dtype) for...  33.9 us
    all_to_all x2, starting transfers between devices, shards(): lax.all_to_all(outgoing.reshape(bands, halo_slots, half), 'band', split_a...  27.4 us
    unnamed x84, local copies, waits for them, and re-layouts  19.9 us
    ppermute x14, starting transfers between devices, swap(): return lax.ppermute(values, 'tp', [(0, 1), (1, 0)])  14.3 us
    ppermute x1, waiting for transfers between devices, shards(): from_low = lax.ppermute(high, 'band', up)  5.68 us
    ppermute x1, waiting for transfers between devices, shards(): from_high = lax.ppermute(low, 'band', down)  3.72 us
  transfers between devices with their start and end apart: 18, of which 8 were waited for; matrix products, arithmetic and copies ran while one was open for 6% of the time, Pallas kernels for 11%

profile of v1, /device:TPU:1, one launch (start us, length us, event | category | flops | bytes accessed | tf_op | source)
XLA Modules:
  0.0 167.5 jit_solution(3441781694175849583)
XLA Ops:
  0.0 3.3 %collective-permute-start.1 = (bf16[256,512]{1,0:T(8,128)(2,1)}, bf16[256,512]{1,0:T(8,128)(2,1)S(1)}, u32[]{:S(2)}, u32[]{:S(2)}) collective-permute-start(bf16[256,512]{1,0:T(8,128)(2,1)} %out_own.1), channel_id=1, source_target_pairs={{0,1},{1,0},{2,3},{3,2},{4,5},{5,4},{6,7},{7,6},{8,9},{9,8},{10,11... | collective-permute-start | bytes 786440 | tf_op jit(solution)/shard_map/ppermute | solution.py:133
  3.4 0.1 collective-permute-start
  3.5 1.5 copy.24.x_ref
  4.9 0.1 collective-permute-done.in_other
  5.1 0.7 copy-done.22
  5.8 0.7 copy-done.19
  6.5 0.9 copy-done.14
  7.4 0.9 copy-done.15
  8.4 0.9 copy-done.20
  9.3 0.9 copy-done.21
  10.3 0.9 copy-done.23
  11.2 0.7 copy-done.33
  11.9 5.2 %shard_map.199 = (bf16[1024,256]{1,0:T(8,128)(2,1)}, bf16[1024,256]{1,0:T(8,128)(2,1)S(1)}, bf16[1024,256]{1,0:T(8,128)(2,1)}) custom-call(bf16[1024,474]{1,0:T(8,128)(2,1)S(1)} %copy.24.x_ref, bf16[474,256]{1,0:T(8,128)(2,1)S(1)} %copy-done.21, bf16[474,256]{1,0:T(8,128)(2,1)S(1)} %copy-done.23, bf16[256,512]{1,0:T(8,128)(2,1)S(1)} %copy-done.14, ...), custom_call_target="tpu_custom_call" | custom-call | tf_op jit(solution)/shard_map/pallas_call | solution.py:48
  17.1 1.4 collective-permute-start.2
  18.5 1.3 collective-permute-start.3
  19.8 0.7 collective-permute-start.6
  20.6 0.1 collective-permute-start.5
  20.7 0.4 collective-permute-start.7
  21.1 0.7 copy.25
  21.8 0.9 reshape.21.refs_2_
  22.7 0.0 copy-start.36
  22.8 1.2 shard_map.200
  24.0 5.7 %collective-permute-done.2.low = bf16[1024,256]{1,0:T(8,128)(2,1)S(1)} collective-permute-done((bf16[1024,256]{1,0:T(8,128)(2,1)}, bf16[1024,256]{1,0:T(8,128)(2,1)S(1)}, u32[]{:S(2)}, u32[]{:S(2)}) %collective-permute-start.2) | collective-permute-done | bytes 524320 | tf_op jit(solution)/shard_map/ppermute | solution.py:175
  29.7 3.7 %collective-permute-done.3.high = bf16[1024,256]{1,0:T(8,128)(2,1)S(1)} collective-permute-done((bf16[1024,256]{1,0:T(8,128)(2,1)}, bf16[1024,256]{1,0:T(8,128)(2,1)S(1)}, u32[]{:S(2)}, u32[]{:S(2)}) %collective-permute-start.3) | collective-permute-done | bytes 524320 | tf_op jit(solution)/shard_map/ppermute | solution.py:176
  33.4 1.6 shard_map.201.hidden_own
  35.1 1.6 collective-permute-start.4
  36.7 0.9 slice_bitcast_fusion.5
  37.6 0.1 collective-permute-done.4.hidden_other
  37.7 4.3 %shard_map.202 = (bf16[320,512]{1,0:T(8,128)(2,1)S(1)}, bf16[320,256]{1,0:T(8,128)(2,1)S(1)}, bf16[320,256]{1,0:T(8,128)(2,1)S(1)}, bf16[2048,256]{1,0:T(8,128)(2,1)}) custom-call(bf16[320,512]{1,0:T(8,128)(2,1)S(1)} %copy-done.2, bf16[320,256]{1,0:T(8,128)(2,1)S(1)} %shard_map.201.hidden_own, bf16[320,256]{1,0:T(8,128)(2,1)S(1)} %collective-permute-done.4.hidden_other, ...), custom_call_target="tpu_custom_call" | custom-call | tf_op jit(solution)/shard_map/pallas_call | solution.py:48
  42.1 0.7 copy-done.24
  42.7 0.7 copy-done.26
  43.4 0.7 copy-done.10
  44.1 19.8 %all-to-all-start = ((bf16[128,16,256]{2,1,0:T(8,128)(2,1)}), bf16[128,16,256]{2,1,0:T(8,128)(2,1)}, u32[]{:S(2)}, u32[]{:S(2)}) async-start(bf16[128,16,256]{2,1,0:T(8,128)(2,1)} %bitcast.3), calls=%async_computation | async-start | bytes 2097152 | tf_op jit(solution)/shard_map/all_to_all | solution.py:201
  64.0 0.0 copy-start.38
  64.0 2.2 %slice_bitcast_fusion = (bf16[1024,256]{1,0:T(8,128)(2,1)}, bf16[1024,256]{1,0:T(8,128)(2,1)S(1)}) fusion(bf16[2,1024,256]{2,1,0:T(8,128)(2,1)} %param.40), kind=kLoop, calls=%fused_computation | loop fusion | bytes 2097152 | tf_op jit(solution)/shard_map/squeeze | solution.py:208
  66.2 0.6 collective-permute-start.10
  66.9 1.8 %slice_bitcast_fusion.2 = (bf16[256,512]{1,0:T(8,128)(2,1)S(1)}, bf16[256,512]{1,0:T(8,128)(2,1)}) fusion(bf16[2,256,512]{2,1,0:T(8,128)(2,1)} %param.41), kind=kLoop, calls=%fused_computation.2 | loop fusion | bytes 1048576 | tf_op jit(solution)/shard_map/squeeze | solution.py:208
  68.7 0.8 slice_bitcast_fusion.3
  69.5 0.5 collective-permute-start.9
  70.0 0.8 slice_bitcast_fusion.4
  70.8 21.8 %all-to-all-done = bf16[128,16,256]{2,1,0:T(8,128)(2,1)} async-done(((bf16[128,16,256]{2,1,0:T(8,128)(2,1)}), bf16[128,16,256]{2,1,0:T(8,128)(2,1)}, u32[]{:S(2)}, u32[]{:S(2)}) %all-to-all-start) | async-done | bytes 1048608 | tf_op jit(solution)/shard_map/all_to_all | solution.py:201
  92.6 0.9 copy-done.6
  93.6 0.9 copy-done.25
  94.5 0.9 copy-done.27
  95.4 7.4 %shard_map.203.hidden_own = bf16[320,256]{1,0:T(8,128)(2,1)S(1)} custom-call(bf16[2560,512]{1,0:T(8,128)(2,1)S(1)} %copy-done, bf16[512,256]{1,0:T(8,128)(2,1)S(1)} %copy-done.6, bf16[320,256]{1,0:T(8,128)(2,1)S(1)} %copy-done.25, bf16[2048,256]{1,0:T(8,128)(2,1)} %bitcast.4.arrived, bf16[320,256]{1,0:T(8,128)(2,1)S(1)} %copy-done.27, ...), custom_call_target="tpu_custom_call" | custom-call | tf_op jit(solution)/shard_map/pallas_call | solution.py:48
  102.8 3.2 %collective-permute-start.8 = (bf16[320,256]{1,0:T(8,128)(2,1)S(1)}, bf16[320,256]{1,0:T(8,128)(2,1)S(1)}, u32[]{:S(2)}, u32[]{:S(2)}) collective-permute-start(bf16[320,256]{1,0:T(8,128)(2,1)S(1)} %shard_map.203.hidden_own), channel_id=1, source_target_pairs={{0,1},{1,0},{2,3},{3,2},{4,5},{5,4},{6,7},{7,6},{8,9},{9,8},{10,11... | collective-permute-start | bytes 491528 | tf_op jit(solution)/shard_map/ppermute | solution.py:133
  106.0 1.0 collective-permute-done.8.hidden_other
  107.0 3.6 %shard_map.204 = (bf16[320,512]{1,0:T(8,128)(2,1)S(1)}, bf16[320,256]{1,0:T(8,128)(2,1)S(1)}, bf16[320,256]{1,0:T(8,128)(2,1)S(1)}, bf16[2048,256]{1,0:T(8,128)(2,1)S(1)}) custom-call(bf16[320,512]{1,0:T(8,128)(2,1)S(1)} %copy-done.11, bf16[320,256]{1,0:T(8,128)(2,1)S(1)} %shard_map.203.hidden_own, bf16[320,256]{1,0:T(8,128)(2,1)S(1)} %collective-permute-done.8.hidden_other, ...), custom_call_target="tpu_custom_call" | custom-call | tf_op jit(solution)/shard_map/pallas_call | solution.py:48
  110.7 1.0 copy-done.3
  111.6 0.7 copy-done.12
  112.4 0.7 copy-done.28
  113.0 0.7 copy-done.30
  113.7 7.5 %all-to-all-start.1 = ((bf16[128,16,256]{2,1,0:T(8,128)(2,1)}), bf16[128,16,256]{2,1,0:T(8,128)(2,1)}, u32[]{:S(2)}, u32[]{:S(2)}) async-start(bf16[128,16,256]{2,1,0:T(8,128)(2,1)} %bitcast.28), calls=%async_computation.1 | async-start | bytes 2097152 | tf_op jit(solution)/shard_map/all_to_all | solution.py:201
  121.3 0.5 collective-permute-start.14
  121.7 0.1 collective-permute-start.13
  121.9 0.4 collective-permute-start.15
  122.3 28.1 %all-to-all-done.1 = bf16[128,16,256]{2,1,0:T(8,128)(2,1)} async-done(((bf16[128,16,256]{2,1,0:T(8,128)(2,1)}), bf16[128,16,256]{2,1,0:T(8,128)(2,1)}, u32[]{:S(2)}, u32[]{:S(2)}) %all-to-all-start.1) | async-done | bytes 1048608 | tf_op jit(solution)/shard_map/all_to_all | solution.py:201
  150.4 1.0 copy-done.5
  151.4 0.9 copy-done.29
  152.3 0.9 copy-done.31
  153.2 7.4 %shard_map.205.hidden_own = bf16[320,256]{1,0:T(8,128)(2,1)S(1)} custom-call(bf16[2560,512]{1,0:T(8,128)(2,1)S(1)} %copy-done, bf16[512,256]{1,0:T(8,128)(2,1)S(1)} %copy-done.5, bf16[320,256]{1,0:T(8,128)(2,1)S(1)} %copy-done.29, bf16[2048,256]{1,0:T(8,128)(2,1)} %bitcast.12.arrived, bf16[320,256]{1,0:T(8,128)(2,1)S(1)} %copy-done.31, ...), custom_call_target="tpu_custom_call" | custom-call | tf_op jit(solution)/shard_map/pallas_call | solution.py:48
  160.6 2.8 %collective-permute-start.12 = (bf16[320,256]{1,0:T(8,128)(2,1)S(1)}, bf16[320,256]{1,0:T(8,128)(2,1)S(1)}, u32[]{:S(2)}, u32[]{:S(2)}) collective-permute-start(bf16[320,256]{1,0:T(8,128)(2,1)S(1)} %shard_map.205.hidden_own), channel_id=1, source_target_pairs={{0,1},{1,0},{2,3},{3,2},{4,5},{5,4},{6,7},{7,6},{8,9},{9,8},{10,11... | collective-permute-start | bytes 491528 | tf_op jit(solution)/shard_map/ppermute | solution.py:133
  163.4 1.0 collective-permute-done.12.hidden_other
  164.4 3.1 %shard_map.206 = bf16[320,512]{1,0:T(8,128)(2,1)} custom-call(bf16[320,512]{1,0:T(8,128)(2,1)S(1)} %copy-done.13, bf16[320,256]{1,0:T(8,128)(2,1)S(1)} %shard_map.205.hidden_own, bf16[320,256]{1,0:T(8,128)(2,1)S(1)} %collective-permute-done.12.hidden_other, bf16[256,512]{1,0:T(8,128)(2,1)S(1)} %copy-done.4, ...), custom_call_target="tpu_custom_call" | custom-call | tf_op jit(solution)/shard_map/pallas_call | solution.py:48
  (72 shorter events, 0.2 us)
Async XLA Ops:
  0.0 19.8 %copy-start.9 = (bf16[1024,256]{1,0:T(8,128)(2,1)S(1)}, bf16[1024,256]{1,0:T(8,128)(2,1)}, u32[]{:S(2)}) copy-start(bf16[1024,256]{1,0:T(8,128)(2,1)} %first_own.1) | copy-start | bytes 1572868
  0.0 20.6 %copy-start.17 = (bf16[256,512]{1,0:T(8,128)(2,1)S(1)}, bf16[256,512]{1,0:T(8,128)(2,1)}, u32[]{:S(2)}) copy-start(bf16[256,512]{1,0:T(8,128)(2,1)} %msg_own.1) | copy-start | bytes 786436
  0.0 21.1 %copy-start.40 = (s32[128,16]{0,1:T(8,128)S(1)}, s32[128,16]{0,1:T(8,128)}, u32[]{:S(2)}) copy-start(s32[128,16]{0,1:T(8,128)} %param.26) | copy-start | bytes 24580
  0.0 22.8 %copy-start.2 = (bf16[320,512]{1,0:T(8,128)(2,1)S(1)}, bf16[320,512]{1,0:T(8,128)(2,1)}, u32[]{:S(2)}) copy-start(bf16[320,512]{1,0:T(8,128)(2,1)} %latent.3) | copy-start | bytes 983044
  0.0 22.8 %copy-start.32 = (s32[3,1024]{1,0:T(4,128)S(1)}, s32[3,1024]{1,0:T(4,128)}, u32[]{:S(2)}) copy-start(s32[3,1024]{1,0:T(4,128)} %slots.5) | copy-start | bytes 36868
  0.0 22.8 %copy-start.16 = (bf16[512,256]{1,0:T(8,128)(2,1)S(1)}, bf16[512,256]{1,0:T(8,128)(2,1)}, u32[]{:S(2)}) copy-start(bf16[512,256]{1,0:T(8,128)(2,1)} %receiver_w.1) | copy-start | bytes 786436
  0.0 5.7 %collective-permute-start.1 = (bf16[256,512]{1,0:T(8,128)(2,1)}, bf16[256,512]{1,0:T(8,128)(2,1)S(1)}, u32[]{:S(2)}, u32[]{:S(2)}) collective-permute-start(bf16[256,512]{1,0:T(8,128)(2,1)} %out_own.1), channel_id=1, source_target_pairs={{0,1},{1,0},{2,3},{3,2},{4,5},{5,4},{6,7},{7,6},{8,9},{9,8},{10,11... | collective-permute-start | bytes 786440 | tf_op jit(solution)/shard_map/ppermute | solution.py:133
  3.4 1.7 %collective-permute-start = (bf16[474,256]{1,0:T(8,128)(2,1)}, bf16[474,256]{1,0:T(8,128)(2,1)S(1)}, u32[]{:S(2)}, u32[]{:S(2)}) collective-permute-start(bf16[474,256]{1,0:T(8,128)(2,1)} %in_own.1), channel_id=1, source_target_pairs={{0,1},{1,0},{2,3},{3,2},{4,5},{5,4},{6,7},{7,6},{8,9},{9,8},{10,11... | collective-permute-start | bytes 728072 | tf_op jit(solution)/shard_map/ppermute | solution.py:133
  5.1 0.7 copy-start.22
  5.8 0.7 copy-start.19
  6.5 0.9 copy-start.14
  7.4 0.9 copy-start.15
  8.4 0.9 copy-start.20
  9.3 0.9 copy-start.21
  10.3 0.9 copy-start.23
  11.2 0.7 copy-start.33
  17.1 12.6 %collective-permute-start.2 = (bf16[1024,256]{1,0:T(8,128)(2,1)}, bf16[1024,256]{1,0:T(8,128)(2,1)S(1)}, u32[]{:S(2)}, u32[]{:S(2)}) collective-permute-start(bf16[1024,256]{1,0:T(8,128)(2,1)} %get-tuple-element.21), channel_id=1, source_target_pairs={{0,2},{2,4},{4,6},{6,8},{8,10},{10,12},{12,14},{14,16},{16,18},{18... | collective-permute-start | bytes 1572872 | tf_op jit(solution)/shard_map/ppermute | solution.py:175
  18.5 14.9 %collective-permute-start.3 = (bf16[1024,256]{1,0:T(8,128)(2,1)}, bf16[1024,256]{1,0:T(8,128)(2,1)S(1)}, u32[]{:S(2)}, u32[]{:S(2)}) collective-permute-start(bf16[1024,256]{1,0:T(8,128)(2,1)} %get-tuple-element.22), channel_id=1, source_target_pairs={{2,0},{4,2},{6,4},{8,6},{10,8},{12,10},{14,12},{16,14},{18,16},{20... | collective-permute-start | bytes 1572872 | tf_op jit(solution)/shard_map/ppermute | solution.py:176
  19.8 17.8 %collective-permute-start.6 = (bf16[1024,256]{1,0:T(8,128)(2,1)S(1)}, bf16[1024,256]{1,0:T(8,128)(2,1)S(1)}, u32[]{:S(2)}, u32[]{:S(2)}) collective-permute-start(bf16[1024,256]{1,0:T(8,128)(2,1)S(1)} %copy-done.9), channel_id=1, source_target_pairs={{0,1},{1,0},{2,3},{3,2},{4,5},{5,4},{6,7},{7,6},{8,9},{9,8},{10,11... | collective-permute-start | bytes 1572872 | tf_op jit(solution)/shard_map/ppermute | solution.py:133
  20.6 17.0 %collective-permute-start.5 = (bf16[256,512]{1,0:T(8,128)(2,1)S(1)}, bf16[256,512]{1,0:T(8,128)(2,1)}, u32[]{:S(2)}, u32[]{:S(2)}) collective-permute-start(bf16[256,512]{1,0:T(8,128)(2,1)S(1)} %copy-done.17), channel_id=1, source_target_pairs={{0,1},{1,0},{2,3},{3,2},{4,5},{5,4},{6,7},{7,6},{8,9},{9,8},{10,11... | collective-permute-start | bytes 786440 | tf_op jit(solution)/shard_map/ppermute | solution.py:133
  20.7 16.9 %collective-permute-start.7 = (bf16[256,512]{1,0:T(8,128)(2,1)}, bf16[256,512]{1,0:T(8,128)(2,1)}, u32[]{:S(2)}, u32[]{:S(2)}) collective-permute-start(bf16[256,512]{1,0:T(8,128)(2,1)} %second_own.1), channel_id=1, source_target_pairs={{0,1},{1,0},{2,3},{3,2},{4,5},{5,4},{6,7},{7,6},{8,9},{9,8},{10,11... | collective-permute-start | bytes 786440 | tf_op jit(solution)/shard_map/ppermute | solution.py:133
  22.7 14.0 %copy-start.36 = (bf16[2,512,256]{2,1,0:T(8,128)(2,1)S(1)}, bf16[2,512,256]{2,1,0:T(8,128)(2,1)}, u32[]{:S(2)}) copy-start(bf16[2,512,256]{2,1,0:T(8,128)(2,1)} %param.37) | copy-start | bytes 1572868
  22.8 14.0 %copy-start.37 = (bf16[2,512,256]{2,1,0:T(8,128)(2,1)S(1)}, bf16[2,512,256]{2,1,0:T(8,128)(2,1)}, u32[]{:S(2)}) copy-start(bf16[2,512,256]{2,1,0:T(8,128)(2,1)} %param.36) | copy-start | bytes 1572868
  22.8 15.0 %copy-start.18 = (bf16[256,512]{1,0:T(8,128)(2,1)S(1)}, bf16[256,512]{1,0:T(8,128)(2,1)}, u32[]{:S(2)}) copy-start(bf16[256,512]{1,0:T(8,128)(2,1)} %second_own.1) | copy-start | bytes 786436
  35.1 2.6 %collective-permute-start.4 = (bf16[320,256]{1,0:T(8,128)(2,1)S(1)}, bf16[320,256]{1,0:T(8,128)(2,1)S(1)}, u32[]{:S(2)}, u32[]{:S(2)}) collective-permute-start(bf16[320,256]{1,0:T(8,128)(2,1)S(1)} %shard_map.201.hidden_own), channel_id=1, source_target_pairs={{0,1},{1,0},{2,3},{3,2},{4,5},{5,4},{6,7},{7,6},{8,9},{9,8},{10,11... | collective-permute-start | bytes 491528 | tf_op jit(solution)/shard_map/ppermute | solution.py:133
  42.1 0.7 copy-start.24
  42.7 0.7 copy-start.26
  43.4 0.7 copy-start.10
  44.1 48.5 %all-to-all-start = ((bf16[128,16,256]{2,1,0:T(8,128)(2,1)}), bf16[128,16,256]{2,1,0:T(8,128)(2,1)}, u32[]{:S(2)}, u32[]{:S(2)}) async-start(bf16[128,16,256]{2,1,0:T(8,128)(2,1)} %bitcast.3), calls=%async_computation | async-start | bytes 2097152 | tf_op jit(solution)/shard_map/all_to_all | solution.py:201
  64.0 4.7 %copy-start.34 = (bf16[2,256,512]{2,1,0:T(8,128)(2,1)S(1)}, bf16[2,256,512]{2,1,0:T(8,128)(2,1)}, u32[]{:S(2)}) copy-start(bf16[2,256,512]{2,1,0:T(8,128)(2,1)} %param.39) | copy-start | bytes 1572868
  64.0 6.0 %copy-start.35 = (bf16[2,512,256]{2,1,0:T(8,128)(2,1)S(1)}, bf16[2,512,256]{2,1,0:T(8,128)(2,1)}, u32[]{:S(2)}) copy-start(bf16[2,512,256]{2,1,0:T(8,128)(2,1)} %param.38) | copy-start | bytes 1572868
  64.0 6.8 %copy-start.38 = (s32[2560]{0:T(1024)S(1)}, s32[2560]{0:T(1024)}, u32[]{:S(2)}) copy-start(s32[2560]{0:T(1024)} %param.27) | copy-start | bytes 30724
  64.0 6.8 %copy-start.39 = (s32[2560]{0:T(1024)S(1)}, s32[2560]{0:T(1024)}, u32[]{:S(2)}) copy-start(s32[2560]{0:T(1024)} %param.28) | copy-start | bytes 30724
  64.0 28.6 %copy-start = (bf16[2560,512]{1,0:T(8,128)(2,1)S(1)}, bf16[2560,512]{1,0:T(8,128)(2,1)}, u32[]{:S(2)}) copy-start(bf16[2560,512]{1,0:T(8,128)(2,1)} %edges.3) | copy-start | bytes 7864324
  66.2 39.8 %collective-permute-start.10 = (bf16[1024,256]{1,0:T(8,128)(2,1)S(1)}, bf16[1024,256]{1,0:T(8,128)(2,1)}, u32[]{:S(2)}, u32[]{:S(2)}) collective-permute-start(bf16[1024,256]{1,0:T(8,128)(2,1)S(1)} %get-tuple-element.32.first_own), channel_id=1, source_target_pairs={{0,1},{1,0},{2,3},{3,2},{4,5},{5,4},{6,7},{7,6},{8,9},{9,8},{10,11... | collective-permute-start | bytes 1572872 | tf_op jit(solution)/shard_map/ppermute | solution.py:133
  68.6 37.3 %collective-permute-start.11 = (bf16[256,512]{1,0:T(8,128)(2,1)}, bf16[256,512]{1,0:T(8,128)(2,1)}, u32[]{:S(2)}, u32[]{:S(2)}) collective-permute-start(bf16[256,512]{1,0:T(8,128)(2,1)} %get-tuple-element.34.second_own), channel_id=1, source_target_pairs={{0,1},{1,0},{2,3},{3,2},{4,5},{5,4},{6,7},{7,6},{8,9},{9,8},{10,11... | collective-permute-start | bytes 786440 | tf_op jit(solution)/shard_map/ppermute | solution.py:133
  69.5 36.5 %collective-permute-start.9 = (bf16[256,512]{1,0:T(8,128)(2,1)}, bf16[256,512]{1,0:T(8,128)(2,1)}, u32[]{:S(2)}, u32[]{:S(2)}) collective-permute-start(bf16[256,512]{1,0:T(8,128)(2,1)} %get-tuple-element.36.msg_own), channel_id=1, source_target_pairs={{0,1},{1,0},{2,3},{3,2},{4,5},{5,4},{6,7},{7,6},{8,9},{9,8},{10,11... | collective-permute-start | bytes 786440 | tf_op jit(solution)/shard_map/ppermute | solution.py:133
  92.6 1.0 copy-start.6
  93.6 0.9 copy-start.25
  94.5 0.9 copy-start.27
  95.4 11.6 %copy-start.7 = (bf16[512,256]{1,0:T(8,128)(2,1)S(1)}, bf16[512,256]{1,0:T(8,128)(2,1)}, u32[]{:S(2)}) copy-start(bf16[512,256]{1,0:T(8,128)(2,1)} %get-tuple-element.39.refs_1_) | copy-start | bytes 786436
  95.4 11.6 %copy-start.8 = (bf16[512,256]{1,0:T(8,128)(2,1)S(1)}, bf16[512,256]{1,0:T(8,128)(2,1)}, u32[]{:S(2)}) copy-start(bf16[512,256]{1,0:T(8,128)(2,1)} %get-tuple-element.44.refs_0_) | copy-start | bytes 786436
  95.4 11.6 %copy-start.11 = (bf16[320,512]{1,0:T(8,128)(2,1)S(1)}, bf16[320,512]{1,0:T(8,128)(2,1)}, u32[]{:S(2)}) copy-start(bf16[320,512]{1,0:T(8,128)(2,1)} %copy-done.10) | copy-start | bytes 983044
  102.8 4.2 %collective-permute-start.8 = (bf16[320,256]{1,0:T(8,128)(2,1)S(1)}, bf16[320,256]{1,0:T(8,128)(2,1)S(1)}, u32[]{:S(2)}, u32[]{:S(2)}) collective-permute-start(bf16[320,256]{1,0:T(8,128)(2,1)S(1)} %shard_map.203.hidden_own), channel_id=1, source_target_pairs={{0,1},{1,0},{2,3},{3,2},{4,5},{5,4},{6,7},{7,6},{8,9},{9,8},{10,11... | collective-permute-start | bytes 491528 | tf_op jit(solution)/shard_map/ppermute | solution.py:133
  110.7 1.0 copy-start.3
  111.6 0.7 copy-start.12
  112.4 0.7 copy-start.28
  113.0 0.7 copy-start.30
  113.7 36.7 %all-to-all-start.1 = ((bf16[128,16,256]{2,1,0:T(8,128)(2,1)}), bf16[128,16,256]{2,1,0:T(8,128)(2,1)}, u32[]{:S(2)}, u32[]{:S(2)}) async-start(bf16[128,16,256]{2,1,0:T(8,128)(2,1)} %bitcast.28), calls=%async_computation.1 | async-start | bytes 2097152 | tf_op jit(solution)/shard_map/all_to_all | solution.py:201
  121.3 43.1 %copy-start.1 = (bf16[1024,256]{1,0:T(8,128)(2,1)S(1)}, bf16[1024,256]{1,0:T(8,128)(2,1)}, u32[]{:S(2)}) copy-start(bf16[1024,256]{1,0:T(8,128)(2,1)} %get-tuple-element.31.first_own) | copy-start | bytes 1572868
  121.3 42.1 %collective-permute-start.14 = (bf16[1024,256]{1,0:T(8,128)(2,1)}, bf16[1024,256]{1,0:T(8,128)(2,1)}, u32[]{:S(2)}, u32[]{:S(2)}) collective-permute-start(bf16[1024,256]{1,0:T(8,128)(2,1)} %get-tuple-element.31.first_own), channel_id=1, source_target_pairs={{0,1},{1,0},{2,3},{3,2},{4,5},{5,4},{6,7},{7,6},{8,9},{9,8},{10,11... | collective-permute-start | bytes 1572872 | tf_op jit(solution)/shard_map/ppermute | solution.py:133
  121.7 41.6 %collective-permute-start.13 = (bf16[256,512]{1,0:T(8,128)(2,1)}, bf16[256,512]{1,0:T(8,128)(2,1)}, u32[]{:S(2)}, u32[]{:S(2)}) collective-permute-start(bf16[256,512]{1,0:T(8,128)(2,1)} %get-tuple-element.35.msg_own), channel_id=1, source_target_pairs={{0,1},{1,0},{2,3},{3,2},{4,5},{5,4},{6,7},{7,6},{8,9},{9,8},{10,11... | collective-permute-start | bytes 786440 | tf_op jit(solution)/shard_map/ppermute | solution.py:133
  121.9 41.5 %collective-permute-start.15 = (bf16[256,512]{1,0:T(8,128)(2,1)S(1)}, bf16[256,512]{1,0:T(8,128)(2,1)}, u32[]{:S(2)}, u32[]{:S(2)}) collective-permute-start(bf16[256,512]{1,0:T(8,128)(2,1)S(1)} %get-tuple-element.33.second_own), channel_id=1, source_target_pairs={{0,1},{1,0},{2,3},{3,2},{4,5},{5,4},{6,7},{7,6},{8,9},{9,8},{10,11... | collective-permute-start | bytes 786440 | tf_op jit(solution)/shard_map/ppermute | solution.py:133
  150.4 14.0 %copy-start.4 = (bf16[256,512]{1,0:T(8,128)(2,1)S(1)}, bf16[256,512]{1,0:T(8,128)(2,1)}, u32[]{:S(2)}) copy-start(bf16[256,512]{1,0:T(8,128)(2,1)} %get-tuple-element.35.msg_own) | copy-start | bytes 786436
  150.4 1.0 copy-start.5
  151.4 0.9 copy-start.29
  152.3 0.9 copy-start.31
  153.2 11.2 %copy-start.13 = (bf16[320,512]{1,0:T(8,128)(2,1)S(1)}, bf16[320,512]{1,0:T(8,128)(2,1)}, u32[]{:S(2)}) copy-start(bf16[320,512]{1,0:T(8,128)(2,1)} %copy-done.12) | copy-start | bytes 983044
  160.6 3.8 %collective-permute-start.12 = (bf16[320,256]{1,0:T(8,128)(2,1)S(1)}, bf16[320,256]{1,0:T(8,128)(2,1)S(1)}, u32[]{:S(2)}, u32[]{:S(2)}) collective-permute-start(bf16[320,256]{1,0:T(8,128)(2,1)S(1)} %shard_map.205.hidden_own), channel_id=1, source_target_pairs={{0,1},{1,0},{2,3},{3,2},{4,5},{5,4},{6,7},{7,6},{8,9},{9,8},{10,11... | collective-permute-start | bytes 491528 | tf_op jit(solution)/shard_map/ppermute | solution.py:133
